TPU v7x, 32 devices: a whole 2x2x4 slice. The times are simulated.
32 devices in a mesh: groups: 2 (over y), row: 16 (over z, x, core).
Axes of the slice: x: 2, y: 2, z: 4, core: 2. Of those that a mesh axis runs over, the one named last changes fastest.
Arguments:
- features: bfloat16 [32768, 256], P(('groups', 'row')), parts along dimension 0, may hold values from -6 to 6
- tile_values: bfloat16 [2048, 128, 128], P(('groups', 'row')), parts along dimension 0, may hold values from -0.16992188 to 0.16992188
- tile_rows: int32 [2048], P(('groups', 'row')), parts along dimension 0, may hold values from -1 to 7, as said below
- tile_cols: int32 [2048], P(('groups', 'row')), parts along dimension 0, may hold values from 0 to 127, as said below
- bias: float32 [256], replicated, may hold values from -3 to 3
- weight: bfloat16 [256, 256], replicated, may hold values from -0.375 to 0.375
- cotangent: bfloat16 [32768, 256], P(('groups', 'row')), parts along dimension 0, may hold values from -6 to 6
Outputs:
- hidden: bfloat16 [32768, 256], P(('groups', 'row')), parts along dimension 0
- grad_features: bfloat16 [32768, 256], P(('groups', 'row')), parts along dimension 0
- grad_weight: float32 [512, 256], P('groups'), parts along dimension 0
- grad_bias: float32 [512], P('groups'), parts along dimension 0
There are 2 independent parts, one for each index of `groups`. A program takes and returns all parts, laid end to end along the dimension named above; an argument that names none is the same for every part. Nothing has to cross between parts.
Inputs may be any that keep to these rules, and one draw needn't show every extreme that they name: `tile_rows`: row block of a slot's tile among its device's 8 row blocks, or -1 for an unused slot. A device's used slots come first; in every draw some device uses all 64 slots. `tile_cols`: for slots of the device holding row blocks d * 8 onward, the column block lies among the blocks of devices d - 1, d and d + 1 that exist in the slab.
All inputs are finite; a program needn't handle non-finite values.
Results may differ from a plain program's by a relative error of at most 0.0055.
The roundings to bfloat16 on the way count: a program that leaves them out, or rounds other values in their place, can miss the bound.
Values may be sent and summed in bfloat16 or wider, within the bound.
A program may use at most 64 MiB of HBM per device.

v0:
```python
import jax
import jax.numpy as jnp
from jax import lax
from jax.sharding import PartitionSpec as P


def with_halo(cells, sides, width):
    for axis, dim in sides:
        count = lax.axis_size(axis)
        ends = count - 1
        head = lax.slice_in_dim(cells, 0, width, axis=dim)
        tail = lax.slice_in_dim(cells, cells.shape[dim] - width, cells.shape[dim], axis=dim)
        cells = jnp.concatenate(
            [
                lax.ppermute(tail, axis, [(i, (i + 1) % count) for i in range(ends)]),
                cells,
                lax.ppermute(head, axis, [((i + 1) % count, i) for i in range(ends)]),
            ],
            axis=dim,
        )
    return cells


def from_behind(block, axis, distance):
    devices = range(lax.axis_size(axis))
    route = [(i - distance, i) for i in devices if i - distance in devices]
    return lax.ppermute(block, axis, route)


def shards(features, tile_values, tile_rows, tile_cols, bias, weight, cotangent):
    block = tile_values.shape[1]
    rows_n, width = features.shape
    nblock = rows_n // block
    extended = with_halo(features, (("row", 0),), rows_n)
    offset = (lax.axis_index("row") - 1) * nblock
    relative = tile_cols - offset
    blocks = extended.reshape(3 * nblock, block, width)[relative]
    product = jnp.einsum("tab,tbh->tah", tile_values, blocks, preferred_element_type=jnp.float32)
    target = jnp.where(tile_rows >= 0, tile_rows, nblock)
    aggregate = jnp.zeros((nblock + 1, block, width), jnp.float32).at[target].add(product)[:nblock]
    aggregate = aggregate.reshape(rows_n, width).astype(jnp.bfloat16)
    preact = jnp.dot(aggregate, weight, preferred_element_type=jnp.float32) + bias
    hidden = jnp.maximum(preact, 0.0).astype(jnp.bfloat16)
    masked = jnp.where(preact > 0, cotangent, jnp.zeros_like(cotangent))
    local_weight = lax.dot_general(
        aggregate, masked, (((0,), (0,)), ((), ())), preferred_element_type=jnp.float32
    )
    local_bias = jnp.sum(masked.astype(jnp.float32), axis=0)
    grad_weight, grad_bias = lax.psum((local_weight, local_bias), "row")
    grad_agg = jnp.dot(masked, weight.T, preferred_element_type=jnp.float32).astype(jnp.bfloat16)
    grad_blocks = grad_agg.reshape(nblock, block, width)
    valid = tile_rows >= 0
    source = grad_blocks[jnp.clip(tile_rows, 0, nblock - 1)]
    source = jnp.where(valid[:, None, None], source, jnp.zeros_like(source))
    contrib = jnp.einsum("tab,tah->tbh", tile_values, source, preferred_element_type=jnp.float32)
    window = jnp.zeros((3 * nblock, block, width), jnp.float32).at[relative].add(contrib)
    lower_part = window[:nblock]
    own_part = window[nblock : 2 * nblock]
    upper_part = window[2 * nblock :]
    from_above = from_behind(lower_part.astype(jnp.bfloat16), "row", -1)
    from_below = from_behind(upper_part.astype(jnp.bfloat16), "row", 1)
    total = own_part + from_above.astype(jnp.float32) + from_below.astype(jnp.float32)
    grad_features = total.reshape(rows_n, width).astype(jnp.bfloat16)
    return (hidden, grad_features, grad_weight, grad_bias)


def solution(mesh):
    return jax.shard_map(
        shards,
        mesh=mesh,
        in_specs=(
            P(("groups", "row"), None),
            P(("groups", "row"), None, None),
            P(("groups", "row")),
            P(("groups", "row")),
            P(),
            P(),
            P(("groups", "row"), None),
        ),
        out_specs=(
            P(("groups", "row"), None),
            P(("groups", "row"), None),
            P("groups", None),
            P("groups"),
        ),
        check_vma=False,
    )
```

profile of v0, /device:TPU:1, one launch (start us, length us, event | category | flops | bytes accessed | tf_op | source)
XLA Modules:
  0.0 210.3 jit_solution(9001943359163058282)
XLA Ops:
  7.2 0.0 copy-start
  7.2 0.0 all-reduce.2.cloned.1.call-start
  7.2 4.6 %collective-permute-start = (bf16[1024,256]{1,0:T(8,128)(2,1)}, bf16[1024,256]{1,0:T(8,128)(2,1)S(1)}, u32[]{:S(2)}, u32[]{:S(2)}) collective-permute-start(bf16[1024,256]{1,0:T(8,128)(2,1)} %param.7), channel_id=1, source_target_pairs={{0,1},{1,2},{2,3},{3,4},{4,5},{5,6},{6,7},{7,8},{8,9},{9,10},{10,1... | collective-permute-start | bytes 1572872 | tf_op jit(solution)/shard_map/ppermute | solution.py:15
  11.9 1.9 collective-permute-start.1
  13.8 0.7 compare_select_fusion.2
  14.5 0.7 compare_select_fusion.1
  15.2 0.7 broadcast_compare_fusion
  15.8 8.1 %collective-permute-done = bf16[1024,256]{1,0:T(8,128)(2,1)S(1)} collective-permute-done((bf16[1024,256]{1,0:T(8,128)(2,1)}, bf16[1024,256]{1,0:T(8,128)(2,1)S(1)}, u32[]{:S(2)}, u32[]{:S(2)}) %collective-permute-start) | collective-permute-done | bytes 524320 | tf_op jit(solution)/shard_map/ppermute | solution.py:15
  23.9 0.0 collective-permute-done.1
  23.9 2.3 %pad_maximum_fusion = bf16[3072,256]{1,0:T(8,128)(2,1)} fusion(bf16[1024,256]{1,0:T(8,128)(2,1)S(1)} %collective-permute-done.1, bf16[1024,256]{1,0:T(8,128)(2,1)} %param.7, bf16[1024,256]{1,0:T(8,128)(2,1)S(1)} %collective-permute-done), kind=kLoop, calls=%fused_computation.10 | loop fusion | flops 4718592 | bytes 3145728 | tf_op jit(solution)/shard_map/concatenate | solution.py:13
  26.2 4.2 %gather_fusion = bf16[64,128,256]{2,1,0:T(8,128)(2,1)} fusion(bf16[24,128,256]{2,1,0:T(8,128)(2,1)} %bitcast.18, s32[1024]{0:T(1024)S(1)} %pad_clamp_fusion.1), kind=kCustom, calls=%fused_computation | custom fusion | bytes 8388864 | tf_op jit(solution)/shard_map/gather | solution.py:37
  30.4 0.0 copy-done
  30.4 6.7 %convolution_bitcast_fusion = f32[64,128,256]{1,2,0:T(8,128)} fusion(bf16[64,128,256]{2,1,0:T(8,128)(2,1)} %gather_fusion, bf16[64,128,128]{2,1,0:T(8,128)(2,1)S(1)} %copy-done), kind=kOutput, calls=%fused_computation.7 | convolution fusion | flops 536870912 | bytes 14680064 | tf_op jit(solution)/shard_map/tab,tbh->tah/dot_general | solution.py:38
  37.1 9.0 %copy.14 = f32[64,128,256]{2,1,0:T(8,128)} copy(f32[64,128,256]{1,2,0:T(8,128)} %convolution_bitcast_fusion) | data formatting | bytes 16777216 | tf_op jit(solution)/shard_map/tab,tbh->tah/dot_general | solution.py:38
  46.1 0.1 broadcast_in_dim.36
  46.2 0.0 copy-start.3
  46.2 0.0 copy-start.5
  46.2 12.3 %scatter_fusion = f32[9,128,256]{2,1,0:T(8,128)S(1)} fusion(f32[9,128,256]{2,1,0:T(8,128)S(1)} %broadcast_in_dim.36, s32[64]{0:T(128)S(1)} %get-tuple-element.9, f32[64,128,256]{2,1,0:T(8,128)} %copy.14), kind=kCustom, calls=%fused_computation.2 | custom fusion | flops 2097152 | bytes 25166080 | tf_op jit(solution)/shard_map/scatter-add | solution.py:40
  58.6 0.0 copy-start.4
  58.6 0.1 slice.33
  58.6 0.0 copy-start.1
  58.7 0.8 copy-done.1
  59.4 0.0 copy-done.3
  59.4 0.0 copy-done.5
  59.4 1.1 maximum_convert_fusion
  60.5 0.0 copy-done.4
  60.5 0.2 convert_reduce_fusion
  60.8 0.3 convolution_convert_fusion
  61.1 2.7 %gather_fusion.1 = bf16[64,128,256]{2,1,0:T(8,128)(2,1)} fusion(bf16[8,128,256]{2,1,0:T(8,128)(2,1)S(1)} %bitcast.17, s32[1024]{0:T(1024)S(1)} %pad_clamp_fusion), kind=kCustom, calls=%fused_computation.1 | custom fusion | bytes 8388864 | tf_op jit(solution)/shard_map/gather | solution.py:53
  63.8 6.8 %fusion.3 = f32[64,128,256]{1,2,0:T(8,128)} fusion(bf16[64,128,128]{2,1,0:T(8,128)(2,1)S(1)} %copy-done, bf16[64,128,256]{2,1,0:T(8,128)(2,1)} %gather_fusion.1, pred[64]{0:T(512)(128)(4,1)S(1)} %broadcast_compare_fusion), kind=kOutput, calls=%fused_computation.8 | convolution fusion | flops 538968064 | bytes 14680128 | tf_op jit(solution)/shard_map/tab,tah->tbh/dot_general | solution.py:55
  70.6 9.0 %copy.16 = f32[64,128,256]{2,1,0:T(8,128)} copy(f32[64,128,256]{1,2,0:T(8,128)} %fusion.3) | data formatting | bytes 16777216 | tf_op jit(solution)/shard_map/tab,tah->tbh/dot_general | solution.py:55
  79.6 2.1 %broadcast_in_dim.40 = f32[24,128,256]{2,1,0:T(8,128)} broadcast(f32[]{:T(128)} %constant.9.clone.1), dimensions={} | broadcast | bytes 3145732 | tf_op jit(solution)/shard_map/broadcast_in_dim | solution.py:56
  81.7 19.2 %scatter_fusion.1 = f32[24,128,256]{2,1,0:T(8,128)} fusion(f32[24,128,256]{2,1,0:T(8,128)} %broadcast_in_dim.40, s32[64]{0:T(128)S(1)} %compare_select_fusion.2, f32[64,128,256]{2,1,0:T(8,128)} %copy.16), kind=kCustom, calls=%fused_computation.3 | custom fusion | flops 2097152 | bytes 25166080 | tf_op jit(solution)/shard_map/scatter-add | solution.py:56
  100.9 0.0 copy-start.2
  100.9 2.1 %convert.8 = bf16[24,128,256]{2,1,0:T(8,128)(2,1)S(1)} convert(f32[24,128,256]{2,1,0:T(8,128)} %scatter_fusion.1) | non-fusion elementwise | flops 786432 | bytes 4718592 | tf_op jit(solution)/shard_map/convert.1
  103.1 1.0 fusion.10
  104.1 1.9 collective-permute-start.2
  106.0 4.2 %collective-permute-start.3 = (bf16[8,128,256]{2,1,0:T(8,128)(2,1)}, bf16[8,128,256]{2,1,0:T(8,128)(2,1)}, u32[]{:S(2)}, u32[]{:S(2)}) collective-permute-start(bf16[8,128,256]{2,1,0:T(8,128)(2,1)} %get-tuple-element.7), channel_id=1, source_target_pairs={{0,1},{1,2},{2,3},{3,4},{4,5},{5,6},{6,7},{7,8},{8,9},{9,10},{10,1... | collective-permute-start | bytes 1572872 | tf_op jit(solution)/shard_map/ppermute | solution.py:27
  110.3 0.0 copy-done.2
  110.3 1.0 fusion.11
  111.3 0.0 all-reduce.2.cloned.1.call-update
  111.4 29.9 %psum.15 = f32[256]{0:T(256)} all-reduce(f32[256]{0:T(256)S(1)} %get-tuple-element.4), channel_id=1, replica_groups=mesh['groups'=2,'row'=16] {'row'}, use_global_device_ids=true, to_apply=%region_4.5 | all-reduce | flops 256 | bytes 2048 | tf_op jit(solution)/shard_map/psum | solution.py:49
  141.3 0.0 collective-permute-done.2
  141.3 0.0 collective-permute-done.3
  141.3 2.3 %fusion.8 = bf16[8,128,256]{2,1,0:T(8,128)(2,1)} fusion(f32[24,128,256]{2,1,0:T(8,128)} %scatter_fusion.1, bf16[8,128,256]{2,1,0:T(8,128)(2,1)} %collective-permute-done.3, bf16[8,128,256]{2,1,0:T(8,128)(2,1)S(1)} %collective-permute-done.2), kind=kLoop, calls=%fused_computation.15 | loop fusion | flops 1310720 | bytes 2621440 | tf_op jit(solution)/shard_map/convert_element_type | solution.py:63
  143.6 58.2 %all-reduce.2.cloned.1.call-done = f32[256,256]{1,0:T(8,128)} async-done(((f32[256,256]{1,0:T(8,128)}), f32[256,256]{1,0:T(8,128)}) %all-reduce.2.cloned.1.call-update) | async-done | bytes 262160 | tf_op jit(solution)/shard_map/psum | solution.py:49
  201.8 1.7 copy.22
  (2 shorter events, 0.0 us)
Async XLA Ops:
  7.2 23.2 %copy-start = (bf16[64,128,128]{2,1,0:T(8,128)(2,1)S(1)}, bf16[64,128,128]{2,1,0:T(8,128)(2,1)}, u32[]{:S(2)}) copy-start(bf16[64,128,128]{2,1,0:T(8,128)(2,1)} %param.8) | copy-start | bytes 6291460
  7.2 194.7 %all-reduce.2.cloned.1.call-start = ((), (), s32[]{:S(2)}) async-start(), calls=%async_computation | async-start | bytes 524288 | tf_op jit(solution)/shard_map/psum | solution.py:49
  7.2 16.7 %collective-permute-start = (bf16[1024,256]{1,0:T(8,128)(2,1)}, bf16[1024,256]{1,0:T(8,128)(2,1)S(1)}, u32[]{:S(2)}, u32[]{:S(2)}) collective-permute-start(bf16[1024,256]{1,0:T(8,128)(2,1)} %param.7), channel_id=1, source_target_pairs={{0,1},{1,2},{2,3},{3,4},{4,5},{5,6},{6,7},{7,8},{8,9},{9,10},{10,1... | collective-permute-start | bytes 1572872 | tf_op jit(solution)/shard_map/ppermute | solution.py:15
  11.9 12.0 %collective-permute-start.1 = (bf16[1024,256]{1,0:T(8,128)(2,1)}, bf16[1024,256]{1,0:T(8,128)(2,1)S(1)}, u32[]{:S(2)}, u32[]{:S(2)}) collective-permute-start(bf16[1024,256]{1,0:T(8,128)(2,1)} %param.7), channel_id=1, source_target_pairs={{1,0},{2,1},{3,2},{4,3},{5,4},{6,5},{7,6},{8,7},{9,8},{10,9},{11,1... | collective-permute-start | bytes 1572872 | tf_op jit(solution)/shard_map/ppermute | solution.py:17
  46.2 13.2 %copy-start.3 = (bf16[256,256]{1,0:T(8,128)(2,1)S(1)}, bf16[256,256]{1,0:T(8,128)(2,1)}, u32[]{:S(2)}) copy-start(bf16[256,256]{1,0:T(8,128)(2,1)} %param.12) | copy-start | bytes 393220
  46.2 13.2 %copy-start.5 = (f32[256]{0:T(256)S(1)}, f32[256]{0:T(256)}, u32[]{:S(2)}) copy-start(f32[256]{0:T(256)} %param.11) | copy-start | bytes 3076
  58.6 2.0 copy-start.4
  58.6 0.8 copy-start.1
  100.9 9.4 %copy-start.2 = (bf16[8,128,256]{2,1,0:T(8,128)(2,1)S(1)}, bf16[8,128,256]{2,1,0:T(8,128)(2,1)}, u32[]{:S(2)}) copy-start(bf16[8,128,256]{2,1,0:T(8,128)(2,1)} %copy-done.1) | copy-start | bytes 1572868
  104.1 37.2 %collective-permute-start.2 = (bf16[8,128,256]{2,1,0:T(8,128)(2,1)}, bf16[8,128,256]{2,1,0:T(8,128)(2,1)S(1)}, u32[]{:S(2)}, u32[]{:S(2)}) collective-permute-start(bf16[8,128,256]{2,1,0:T(8,128)(2,1)} %get-tuple-element.6), channel_id=1, source_target_pairs={{1,0},{2,1},{3,2},{4,3},{5,4},{6,5},{7,6},{8,7},{9,8},{10,9},{11,1... | collective-permute-start | bytes 1572872 | tf_op jit(solution)/shard_map/ppermute | solution.py:27
  106.0 35.3 %collective-permute-start.3 = (bf16[8,128,256]{2,1,0:T(8,128)(2,1)}, bf16[8,128,256]{2,1,0:T(8,128)(2,1)}, u32[]{:S(2)}, u32[]{:S(2)}) collective-permute-start(bf16[8,128,256]{2,1,0:T(8,128)(2,1)} %get-tuple-element.7), channel_id=1, source_target_pairs={{0,1},{1,2},{2,3},{3,4},{4,5},{5,6},{6,7},{7,8},{8,9},{9,10},{10,1... | collective-permute-start | bytes 1572872 | tf_op jit(solution)/shard_map/ppermute | solution.py:27
Sparse Core Ops, SparseCore 0:
  111.5 90.3 all-reduce.1
where the time goes:
time: 211 us; the launch traced here: 210 us
  waiting for transfers between devices  66.3 us (31%)
  other arithmetic  40.5 us (19%)
  local copies, waits for them, and re-layouts  30.7 us (15%)
  blocking collectives  29.9 us (14%)
  matrix products  16 us (8%)
  between operations  14.2 us (7%)
  starting transfers between devices  12.8 us (6%)
    psum x1, waiting for transfers between devices, shards(): grad_weight, grad_bias = lax.psum((local_weight, local_bias), 'row')  58.2 us
    psum x1, blocking collectives, shards(): grad_weight, grad_bias = lax.psum((local_weight, local_bias), 'row')  29.9 us
    scatter-add x1, other arithmetic, shards(): jnp.zeros((3 * nblock, block, width), jnp.float32).at[relative].add(contrib)  19.2 us
    scatter-add x1, other arithmetic, shards(): jnp.zeros((nblock + 1, block, width), jnp.float32).at[target].add(product)  12.3 us
    dot_general x1, local copies, waits for them, and re-layouts, shards(): jnp.einsum('tab,tah->tbh', tile_values, source, preferred_element_type=jn...  9.01 us
    dot_general x1, local copies, waits for them, and re-layouts, shards(): jnp.einsum('tab,tbh->tah', tile_values, blocks, preferred_element_type=jn...  9 us
    ppermute x1, waiting for transfers between devices, with_halo(): lax.ppermute(tail, axis, [(i, (i + 1) % count) for i in range(ends)])  8.1 us
    dot_general x1, matrix products, shards(): jnp.einsum('tab,tah->tbh', tile_values, source, preferred_element_type=jn...  6.79 us
  transfers between devices with their start and end apart: 5, of which 2 were waited for; matrix products, arithmetic and copies ran while one was open for 3% of the time, Pallas kernels for 0%

commit v1 on v0

v1 whole, which is shorter than its diff:
```python
import functools

import jax
import jax.numpy as jnp
from jax import lax
from jax.experimental import pallas as pl
from jax.experimental.pallas import tpu as pltpu
from jax.sharding import PartitionSpec as P

MESH = pl.DeviceIdType.MESH
F32 = jnp.float32
BF16 = jnp.bfloat16


def stages_of(count):
    stages = []
    rest = count
    if rest % 2 == 0:
        stages.append((2, 1))
        rest //= 2
    low = count // rest
    while rest > 1:
        size = next(f for f in (4, 2, 3, 5, 7, rest) if rest % f == 0)
        rest //= size
        stages.append((size, low * rest))
    return stages


def splits_of(rows, stages):
    out = []
    for size, stride in stages:
        scatter = rows % (8 * size) == 0
        out.append((size, stride, rows, scatter))
        if scatter:
            rows //= size
    return out


def kernel(
    count, chunk, table, feat, tiles, bias, weight, cot,
    hid_out, gf_out, gw_out, gb_out,
    x, tv, pn, pt, adj, adj_lo, adjt, cv, g, hid, send, recv, own, gw, gwo, gb, rs_in, gb_in,
    local_sem, out_sem, halo_s, halo_r, part_s, part_r, rs_s, rs_r, gb_s, gb_r, ag_s, ag_r,
):
    me = lax.axis_index("row")
    rows, width = cv.shape
    slots, blk, _ = tv.shape
    nblk = rows // blk
    ncol = 3 * nblk
    stages = splits_of(gw.shape[0], stages_of(count))
    up, down = lax.rem(me + 1, count), lax.rem(me + count - 1, count)
    has_up, has_down = me < count - 1, me > 0

    def peer(size, stride, step):
        at = lax.rem(lax.div(me, stride), size)
        other = lax.rem(at + step, size)
        return at, other, me + (other - at) * stride

    cp_tiles = pltpu.make_async_copy(tiles, tv, local_sem.at[0])
    cp_feat = pltpu.make_async_copy(feat, x.at[1], local_sem.at[1])
    cp_cot = pltpu.make_async_copy(cot, cv, local_sem.at[2])
    cp_tiles.start()
    cp_feat.start()
    cp_cot.start()

    barrier = pltpu.get_barrier_semaphore()

    @pl.when(has_up)
    def _():
        pl.semaphore_signal(barrier, inc=1, device_id={"row": up}, device_id_type=MESH)

    @pl.when(has_down)
    def _():
        pl.semaphore_signal(barrier, inc=1, device_id={"row": down}, device_id_type=MESH)

    greeted = 0
    for size, stride, _, _ in stages:
        for step in range(1, size):
            _, _, dev = peer(size, stride, step)
            pl.semaphore_signal(barrier, inc=1, device_id={"row": dev}, device_id_type=MESH)
            greeted += 1
    pl.semaphore_wait(barrier, greeted + has_up.astype(jnp.int32) + has_down.astype(jnp.int32))

    halo_up = pltpu.make_async_remote_copy(
        feat, x.at[0], halo_s.at[0], halo_r.at[0], device_id={"row": up}, device_id_type=MESH)
    halo_down = pltpu.make_async_remote_copy(
        feat, x.at[2], halo_s.at[1], halo_r.at[1], device_id={"row": down}, device_id_type=MESH)

    @pl.when(has_up)
    def _():
        halo_up.start()

    @pl.when(has_down)
    def _():
        halo_down.start()

    @pl.when(jnp.logical_not(has_down))
    def _():
        x[0] = jnp.zeros((rows, width), BF16)
        recv[0] = jnp.zeros((rows, width), BF16)

    @pl.when(jnp.logical_not(has_up))
    def _():
        x[2] = jnp.zeros((rows, width), BF16)
        recv[1] = jnp.zeros((rows, width), BF16)

    pn[0] = jnp.zeros((blk, blk), F32)
    pt[0] = jnp.zeros((blk, blk), F32)
    cp_tiles.wait()

    def add_slot(s, carry):
        total = tv[s].astype(F32) + pn[table[s]]
        pn[s + 1] = total
        pt[s + 1] = total.T
        return carry

    lax.fori_loop(0, slots, add_slot, 0)

    def fill_row(r, carry):
        at = pl.multiple_of(r * blk, blk)
        for c in range(ncol):
            which = table[slots + r * ncol + c]
            cell = pn[which]
            top = cell.astype(BF16)
            adj[pl.ds(at, blk), c * blk:(c + 1) * blk] = top
            adj_lo[pl.ds(at, blk), c * blk:(c + 1) * blk] = (cell - top.astype(F32)).astype(BF16)
            adjt[c * blk:(c + 1) * blk, pl.ds(at, blk)] = pt[which].astype(BF16)
        return carry

    lax.fori_loop(0, nblk, fill_row, 0)

    cp_feat.wait()

    def strip(at, third):
        cols = slice(third * rows, (third + 1) * rows)
        return (jnp.dot(adj[at, cols], x[third], preferred_element_type=F32)
                + jnp.dot(adj_lo[at, cols], x[third], preferred_element_type=F32))

    def own_rows(i, carry):
        at = pl.ds(pl.multiple_of(i * chunk, chunk), chunk)
        own[at, :] = strip(at, 1)
        return carry

    lax.fori_loop(0, rows // chunk, own_rows, 0)

    cp_cot.wait()

    @pl.when(has_down)
    def _():
        halo_up.wait_recv()

    @pl.when(has_up)
    def _():
        halo_down.wait_recv()

    gw[...] = jnp.zeros_like(gw)
    gb[...] = jnp.zeros_like(gb)

    def dense(i, carry):
        at = pl.ds(pl.multiple_of(i * chunk, chunk), chunk)
        agg = (own[at, :] + strip(at, 0) + strip(at, 2)).astype(BF16)
        pre = jnp.dot(agg, weight[...], preferred_element_type=F32) + bias[...]
        hid[at, :] = jnp.maximum(pre, 0.0).astype(BF16)
        masked32 = jnp.where(pre > 0, cv[at, :].astype(F32), 0.0)
        masked = masked32.astype(BF16)
        gw[...] += lax.dot_general(agg, masked, (((0,), (0,)), ((), ())), preferred_element_type=F32)
        gb[...] += jnp.sum(masked32.reshape(chunk // 8, 8, width), axis=0)
        g[at, :] = lax.dot_general(
            masked, weight[...], (((1,), (1,)), ((), ())), preferred_element_type=F32).astype(BF16)
        return carry

    lax.fori_loop(0, rows // chunk, dense, 0)

    cp_hid = pltpu.make_async_copy(hid, hid_out, out_sem.at[0])
    cp_hid.start()

    bases = [0]
    plan = []
    first = 0
    for size, stride, n_rows, scatter in stages:
        plan.append((size, stride, n_rows // size if scatter else n_rows, scatter, first, bases[-1]))
        at = lax.rem(lax.div(me, stride), size)
        bases.append(bases[-1] + at * (n_rows // size) if scatter else bases[-1])
        first += size - 1

    def reduce_copies(k):
        size, stride, sub, scatter, first, base = plan[k]
        found = []
        for step in range(1, size):
            at, other, dev = peer(size, stride, step)
            sem = first + step - 1
            start = pl.multiple_of(base + other * sub, 8) if scatter else base
            found.append(pltpu.make_async_remote_copy(
                gw.at[pl.ds(start, sub)], rs_in.at[sem, pl.ds(0, sub)],
                rs_s.at[sem], rs_r.at[sem], device_id={"row": dev}, device_id_type=MESH))
            found.append(pltpu.make_async_remote_copy(
                gb.at[...], gb_in.at[sem],
                gb_s.at[sem], gb_r.at[sem], device_id={"row": dev}, device_id_type=MESH))
        return found

    def in_order(mine, slot, size, stride, first):
        at = lax.rem(lax.div(me, stride), size)
        total = None
        for member in range(size):
            term = jnp.where(at == member, mine, 0.0)
            for step in range(1, size):
                term = jnp.where(lax.rem(at - step + size, size) == member, slot(first + step - 1), term)
            total = term if total is None else total + term
        return total

    def reduce_finish(k, copies):
        size, stride, sub, scatter, first, base = plan[k]
        for c in copies:
            c.wait()
        start = pl.multiple_of(bases[k + 1], 8) if scatter else base
        here = pl.ds(start, sub)
        if scatter:
            total = gw[here, :]
            for step in range(1, size):
                total = total + rs_in[first + step - 1, :sub]
        else:
            total = in_order(gw[here, :], lambda i: rs_in[i, :sub], size, stride, first)
        gw[here, :] = total
        gb[...] = in_order(gb[...], lambda i: gb_in[i], size, stride, first)

    def gather_copies(k):
        size, stride, sub, scatter, first, base = plan[k]
        found = []
        if scatter:
            here = pl.ds(pl.multiple_of(bases[k + 1], 8), sub)
            for step in range(1, size):
                _, _, dev = peer(size, stride, step)
                sem = first + step - 1
                found.append(pltpu.make_async_remote_copy(
                    gwo.at[here], gwo.at[here],
                    ag_s.at[sem], ag_r.at[sem], device_id={"row": dev}, device_id_type=MESH))
        return found

    copies = reduce_copies(0)
    for c in copies:
        c.start()

    n_chunk = rows // chunk

    def part_copy(i, side):
        at = pl.ds(pl.multiple_of(i * chunk, chunk), chunk)
        return pltpu.make_async_remote_copy(
            send.at[side, at], recv.at[1 - side, at], part_s.at[side, i], part_r.at[side, i],
            device_id={"row": up if side else down}, device_id_type=MESH)

    def parts(i, carry):
        at = pl.multiple_of(i * chunk, chunk)
        for side, has in ((0, has_down), (1, has_up)):
            rows_at = pl.ds(pl.multiple_of(side * 2 * rows + at, chunk), chunk)
            send[side, pl.ds(at, chunk)] = jnp.dot(
                adjt[rows_at, :], g[...], preferred_element_type=F32).astype(BF16)

            @pl.when(has)
            def _():
                part_copy(i, side).start()
        return carry

    lax.fori_loop(0, n_chunk, parts, 0)

    reduce_finish(0, copies)
    if len(plan) > 1:
        copies = reduce_copies(1)
        for c in copies:
            c.start()

    def own_part(i, carry):
        at = pl.multiple_of(i * chunk, chunk)
        rows_at = pl.ds(pl.multiple_of(rows + at, chunk), chunk)
        own[pl.ds(at, chunk), :] = jnp.dot(adjt[rows_at, :], g[...], preferred_element_type=F32)
        return carry

    lax.fori_loop(0, n_chunk, own_part, 0)

    for k in range(1, len(plan)):
        reduce_finish(k, copies)
        if k + 1 < len(plan):
            copies = reduce_copies(k + 1)
            for c in copies:
                c.start()
    mine = pl.ds(pl.multiple_of(bases[-1], 8), plan[-1][2])
    gwo[mine, :] = gw[mine, :]
    cp_gb = pltpu.make_async_copy(gb, gb_out, out_sem.at[1])
    cp_gb.start()
    for k in reversed(range(len(plan))):
        copies = gather_copies(k)
        for c in copies:
            c.start()
        for c in copies:
            c.wait()
    cp_gw = pltpu.make_async_copy(gwo, gw_out, out_sem.at[2])
    cp_gw.start()

    cp_hid.wait()

    def finish(i, carry):
        at = pl.ds(pl.multiple_of(i * chunk, chunk), chunk)

        @pl.when(has_up)
        def _():
            part_copy(i, 0).wait_recv()

        @pl.when(has_down)
        def _():
            part_copy(i, 1).wait_recv()

        hid[at, :] = (own[at, :] + recv[0, at].astype(F32) + recv[1, at].astype(F32)).astype(BF16)
        return carry

    lax.fori_loop(0, n_chunk, finish, 0)
    cp_gf = pltpu.make_async_copy(hid, gf_out, out_sem.at[0])
    cp_gf.start()

    def sent(i, carry):
        @pl.when(has_down)
        def _():
            part_copy(i, 0).wait_send()

        @pl.when(has_up)
        def _():
            part_copy(i, 1).wait_send()
        return carry

    lax.fori_loop(0, n_chunk, sent, 0)

    @pl.when(has_up)
    def _():
        halo_up.wait_send()

    @pl.when(has_down)
    def _():
        halo_down.wait_send()

    cp_gf.wait()
    cp_gb.wait()
    cp_gw.wait()


def shards(count, features, tile_values, tile_rows, tile_cols, bias, weight, cotangent):
    slots, blk, _ = tile_values.shape
    rows, width = features.shape
    nblk = rows // blk
    ncol = 3 * nblk
    chunk = min(256, rows)
    rel = tile_cols - (lax.axis_index("row") - 1) * nblk
    key = jnp.where(tile_rows >= 0, tile_rows * ncol + rel, -1)
    wanted = jnp.concatenate([key, jnp.arange(nblk * ncol, dtype=jnp.int32)])
    limit = jnp.minimum(jnp.arange(slots + nblk * ncol, dtype=jnp.int32), slots)
    slot = jnp.arange(slots, dtype=jnp.int32)
    hit = (key[None, :] == wanted[:, None]) & (slot[None, :] < limit[:, None])
    table = jnp.max(jnp.where(hit, slot[None, :] + 1, 0), axis=1)

    stages = splits_of(width, stages_of(count))
    n_msg = max(1, sum(s[0] - 1 for s in stages))
    biggest = max([s[2] // s[0] if s[3] else s[2] for s in stages] + [8])
    hbm = pl.BlockSpec(memory_space=pl.ANY)
    vmem = pl.BlockSpec(memory_space=pltpu.VMEM)
    dma = pltpu.SemaphoreType.DMA
    hidden, grad_features, grad_weight, grad_bias = pl.pallas_call(
        functools.partial(kernel, count, chunk),
        out_shape=(
            jax.ShapeDtypeStruct((rows, width), BF16),
            jax.ShapeDtypeStruct((rows, width), BF16),
            jax.ShapeDtypeStruct((width, width), F32),
            jax.ShapeDtypeStruct((8, width), F32),
        ),
        in_specs=[pl.BlockSpec(memory_space=pltpu.SMEM), hbm, hbm, vmem, vmem, hbm],
        out_specs=(hbm, hbm, hbm, hbm),
        scratch_shapes=[
            pltpu.VMEM((3, rows, width), BF16),
            pltpu.VMEM((slots, blk, blk), BF16),
            pltpu.VMEM((slots + 1, blk, blk), F32),
            pltpu.VMEM((slots + 1, blk, blk), F32),
            pltpu.VMEM((rows, 3 * rows), BF16),
            pltpu.VMEM((rows, 3 * rows), BF16),
            pltpu.VMEM((3 * rows, rows), BF16),
            pltpu.VMEM((rows, width), BF16),
            pltpu.VMEM((rows, width), BF16),
            pltpu.VMEM((rows, width), BF16),
            pltpu.VMEM((2, rows, width), BF16),
            pltpu.VMEM((2, rows, width), BF16),
            pltpu.VMEM((rows, width), F32),
            pltpu.VMEM((width, width), F32),
            pltpu.VMEM((width, width), F32),
            pltpu.VMEM((8, width), F32),
            pltpu.VMEM((n_msg, biggest, width), F32),
            pltpu.VMEM((n_msg, 8, width), F32),
            dma((3,)),
            dma((3,)),
            dma((2,)),
            dma((2,)),
            dma((2, rows // chunk)),
            dma((2, rows // chunk)),
            dma((n_msg,)),
            dma((n_msg,)),
            dma((n_msg,)),
            dma((n_msg,)),
            dma((n_msg,)),
            dma((n_msg,)),
        ],
        compiler_params=pltpu.CompilerParams(
            collective_id=0, has_side_effects=True, vmem_limit_bytes=48 * 1024 * 1024),
    )(table, features, tile_values, bias.reshape(1, width), weight, cotangent)
    return hidden, grad_features, grad_weight, jnp.sum(grad_bias, axis=0)


def solution(mesh):
    return jax.shard_map(
        functools.partial(shards, mesh.shape["row"]),
        mesh=mesh,
        in_specs=(
            P(("groups", "row"), None),
            P(("groups", "row"), None, None),
            P(("groups", "row")),
            P(("groups", "row")),
            P(),
            P(),
            P(("groups", "row"), None),
        ),
        out_specs=(
            P(("groups", "row"), None),
            P(("groups", "row"), None),
            P("groups", None),
            P("groups"),
        ),
        check_vma=False,
    )
```

time: 211 us -> 55.6 us (0.26)
  waiting for transfers between devices: 66.3 us -> 0 us
  Pallas kernels: 0 us -> 45.6 us
  other arithmetic: 40.5 us -> 1.43 us
  blocking collectives: 29.9 us -> 0 us
  local copies, waits for them, and re-layouts: 30.7 us -> 7.54 us
  matrix products: 16 us -> 0 us
  between operations: 14.2 us -> 0.66 us
  starting transfers between devices: 12.8 us -> 0 us
    psum x1 -> x0, waiting for transfers between devices: 58.2 us -> none  [shards(): grad_weight, grad_bias = lax.psum((local_weight, local_bias), 'row')]
    pallas_call x0 -> x1, Pallas kernels: none -> 45.6 us  [shards(): pl.pallas_call(functools.partial(kernel, count, chunk), out_shape=(jax.Sh...]
    scatter-add x2 -> x0, other arithmetic: 31.5 us -> none  [the longest x1 19.2 us: shards(): jnp.zeros((3 * nblock, block, width), jnp.float32).at[relative].add(contrib)]
    psum x1 -> x0, blocking collectives: 29.9 us -> none  [shards(): grad_weight, grad_bias = lax.psum((local_weight, local_bias), 'row')]
    dot_general x2 -> x0, local copies, waits for them, and re-layouts: 18 us -> none  [the longest x1 9.01 us: shards(): jnp.einsum('tab,tah->tbh', tile_values, source, preferred_element_type=jn...]
    dot_general x5 -> x0, matrix products: 16 us -> none  [the longest x1 6.79 us: shards(): jnp.einsum('tab,tah->tbh', tile_values, source, preferred_element_type=jn...]
    ppermute x4 -> x0, starting transfers between devices: 12.7 us -> none  [the longest x2 6.15 us: from_behind(): return lax.ppermute(block, axis, route)]
    ppermute x4 -> x0, waiting for transfers between devices: 8.11 us -> none  [the longest x1 8.1 us: with_halo(): lax.ppermute(tail, axis, [(i, (i + 1) % count) for i in range(ends)])]
  transfers between devices with their start and end apart: 5 -> 0, of which waited for: 2 -> 0; matrix products, arithmetic and copies ran while one was open for 3% -> 0% of each run, Pallas kernels for 0% -> 0%
where the time goes in v1:
time: 55.6 us; the launch traced here: 55.2 us
  Pallas kernels  45.6 us (82%)
  local copies, waits for them, and re-layouts  7.54 us (14%)
  other arithmetic  1.43 us (3%)
  between operations  0.66 us (1%)
    pallas_call x1, Pallas kernels, shards(): pl.pallas_call(functools.partial(kernel, count, chunk), out_shape=(jax.Sh...  45.6 us
    unnamed x13, local copies, waits for them, and re-layouts  7.54 us

profile of v1, /device:TPU:1, one launch (start us, length us, event | category | flops | bytes accessed | tf_op | source)
XLA Modules:
  0.0 55.2 jit_solution(15001134608701511633)
XLA Ops:
  0.6 0.7 %compare_select_fusion = (s32[64]{0:T(128)S(1)}, s32[64]{0:T(128)S(1)}) fusion(s32[64]{0:T(128)} %param.9, s32[64]{0:T(128)} %param.10, s32[]{:T(128)S(6)} %mul.11), kind=kLoop, calls=%fused_computation.3 | loop fusion | flops 384 | bytes 1028 | tf_op jit(solution)/shard_map/jit(_where)/select_n | solution.py:350
  1.3 0.1 pad_add_fusion
  1.4 0.1 select_reduce_fusion.table
  1.5 0.0 copy-start
  1.5 1.6 %copy-done = bf16[64,128,128]{2,1,0:T(8,128)(2,1)S(1)} copy-done((bf16[64,128,128]{2,1,0:T(8,128)(2,1)S(1)}, bf16[64,128,128]{2,1,0:T(8,128)(2,1)}, u32[]{:S(2)}) %copy-start) | copy-done | bytes 2097176
  3.1 0.0 copy-start.1
  3.1 1.0 %copy-done.1 = bf16[1024,256]{1,0:T(8,128)(2,1)S(1)} copy-done((bf16[1024,256]{1,0:T(8,128)(2,1)S(1)}, bf16[1024,256]{1,0:T(8,128)(2,1)}, u32[]{:S(2)}) %copy-start.1) | copy-done | bytes 524312
  4.1 0.0 copy-start.2
  4.1 1.0 %copy-done.2 = bf16[1024,256]{1,0:T(8,128)(2,1)S(1)} copy-done((bf16[1024,256]{1,0:T(8,128)(2,1)S(1)}, bf16[1024,256]{1,0:T(8,128)(2,1)}, u32[]{:S(2)}) %copy-start.2) | copy-done | bytes 524312
  5.2 0.0 copy-start.3
  5.2 0.9 %copy-done.3 = bf16[256,256]{1,0:T(8,128)(2,1)S(1)} copy-done((bf16[256,256]{1,0:T(8,128)(2,1)S(1)}, bf16[256,256]{1,0:T(8,128)(2,1)}, u32[]{:S(2)}) %copy-start.3) | copy-done | bytes 131096
  6.1 0.0 copy-start.4
  6.1 0.7 %copy-done.4 = f32[256]{0:T(256)S(1)} copy-done((f32[256]{0:T(256)S(1)}, f32[256]{0:T(256)}, u32[]{:S(2)}) %copy-start.4) | copy-done | bytes 1048
  6.8 45.6 %shard_map.102 = (bf16[1024,256]{1,0:T(8,128)(2,1)S(1)}, bf16[1024,256]{1,0:T(8,128)(2,1)S(1)}, f32[256,256]{1,0:T(8,128)S(1)}, f32[8,256]{1,0:T(8,128)S(1)}) custom-call(s32[256]{0:T(256)S(1)} %select_reduce_fusion.table, bf16[1024,256]{1,0:T(8,128)(2,1)S(1)} %copy-done.1, bf16[64,128,128]{2,1,0:T(8,128)(2,1)S(1)} %copy-done, f32[1,256]{1,0:T(1,128)S(1)} %bitcast.1, ...), custom_call_target="tpu_custom_call" | custom-call | tf_op jit(solution)/shard_map/pallas_call | solution.py:363
  52.4 0.6 %reduce_sum.9 = f32[256]{0:T(256)} reduce(f32[8,256]{1,0:T(8,128)S(1)} %get-tuple-element.11, f32[]{:T(128)} %constant.7.clone.1), dimensions={0}, to_apply=%region_1.2 | reduce | flops 1792 | bytes 9220 | tf_op jit(solution)/shard_map/reduce_sum | solution.py:408
  52.9 0.8 %copy.14 = bf16[1024,256]{1,0:T(8,128)(2,1)} copy(bf16[1024,256]{1,0:T(8,128)(2,1)S(1)} %get-tuple-element.18) | data formatting | bytes 1048576
  53.7 0.8 %copy.15 = bf16[1024,256]{1,0:T(8,128)(2,1)} copy(bf16[1024,256]{1,0:T(8,128)(2,1)S(1)} %get-tuple-element.19) | data formatting | bytes 1048576
  54.5 0.7 %copy.16 = f32[256,256]{1,0:T(8,128)} copy(f32[256,256]{1,0:T(8,128)S(1)} %get-tuple-element.20) | data formatting | bytes 524288
  (2 shorter events, 0.0 us)
Async XLA Ops:
  1.5 1.6 %copy-start = (bf16[64,128,128]{2,1,0:T(8,128)(2,1)S(1)}, bf16[64,128,128]{2,1,0:T(8,128)(2,1)}, u32[]{:S(2)}) copy-start(bf16[64,128,128]{2,1,0:T(8,128)(2,1)} %tiles.1) | copy-start | bytes 6291460
  3.1 1.0 %copy-start.1 = (bf16[1024,256]{1,0:T(8,128)(2,1)S(1)}, bf16[1024,256]{1,0:T(8,128)(2,1)}, u32[]{:S(2)}) copy-start(bf16[1024,256]{1,0:T(8,128)(2,1)} %feat.1) | copy-start | bytes 1572868
  4.1 1.0 %copy-start.2 = (bf16[1024,256]{1,0:T(8,128)(2,1)S(1)}, bf16[1024,256]{1,0:T(8,128)(2,1)}, u32[]{:S(2)}) copy-start(bf16[1024,256]{1,0:T(8,128)(2,1)} %cot.1) | copy-start | bytes 1572868
  5.2 0.9 %copy-start.3 = (bf16[256,256]{1,0:T(8,128)(2,1)S(1)}, bf16[256,256]{1,0:T(8,128)(2,1)}, u32[]{:S(2)}) copy-start(bf16[256,256]{1,0:T(8,128)(2,1)} %weight.1) | copy-start | bytes 393220
  6.1 0.7 %copy-start.4 = (f32[256]{0:T(256)S(1)}, f32[256]{0:T(256)}, u32[]{:S(2)}) copy-start(f32[256]{0:T(256)} %param.11) | copy-start | bytes 3076
